TPU v7x, 32 devices: a whole 2x2x4 slice. The times are simulated.
32 devices in a mesh: src: 4 (over y, core), snk: 8 (over z, x).
Axes of the slice: x: 2, y: 2, z: 4, core: 2. Of those that a mesh axis runs over, the one named last changes fastest.
Arguments:
- peram: bfloat16 [4, 8, 2, 256, 256], P('src', None, None, None, 'snk'), may hold values from -6 to 6
- meson_blocks: bfloat16 [8, 4, 2, 256, 256], P('snk'), may hold values from -0.25 to 0.25
- edge_left: int32 [4, 8, 32], P('src', 'snk'), may hold values from 0 to 3
- edge_right: int32 [4, 8, 32], P('src', 'snk'), may hold values from 0 to 3
- edge_node: int32 [4, 8, 32], P('src', 'snk'), may hold values from 0 to 4
- edge_weight: int32 [4, 8, 32], P('src', 'snk'), may hold values from 0 to 15
- weight_table: float32 [16, 2], replicated, may hold values from -0.2 to 0.2
Outputs:
- node_matrices: bfloat16 [256, 4, 2, 256], P('snk')
Inputs may be any that keep to these rules, and one draw needn't show every extreme that they name: `edge_node`: the value 4 marks an empty slot that feeds no node.
All inputs are finite; a program needn't handle non-finite values.
Results may differ from a plain program's by a relative error of at most 0.009.
Values may be sent and summed in bfloat16 or wider, within the bound.
A program may use at most 128 MiB of HBM per device.

v0:
```python
import jax
import jax.numpy as jnp
from jax import lax
from jax.sharding import PartitionSpec as P

NODES = 4
NW = 16


def from_root(value, axis, source):
    kept = jnp.where(lax.axis_index(axis) == source, value, 0).astype(value.dtype)
    return lax.psum(kept, axis)


def block_products(blocks, whole_peram):
    number = blocks.shape[0]
    order = blocks.shape[2]
    left_real = blocks[:, 0].reshape(number * order, order)
    left_imag = blocks[:, 1].reshape(number * order, order)
    real_part = jnp.dot(left_real, whole_peram[0], preferred_element_type=jnp.float32) - jnp.dot(
        left_imag, whole_peram[1], preferred_element_type=jnp.float32
    )
    imag_part = jnp.dot(left_real, whole_peram[1], preferred_element_type=jnp.float32) + jnp.dot(
        left_imag, whole_peram[0], preferred_element_type=jnp.float32
    )
    stacked = jnp.stack(
        [real_part.reshape(number, order, order), imag_part.reshape(number, order, order)], 1
    )
    return stacked.astype(jnp.bfloat16)


def shards(peram, meson_blocks, edge_left, edge_right, edge_node, edge_weight, weight_table):
    high = lax.Precision.HIGHEST
    src_total = lax.axis_size("src")
    snk_total = lax.axis_size("snk")
    whole_peram = lax.all_to_all(peram, "snk", split_axis=1, concat_axis=4, tiled=True)[0, 0]
    source_root = lax.axis_index("src") * (snk_total // src_total)
    right_all = from_root(meson_blocks, "snk", source_root)[0]
    left_all = meson_blocks[0]
    left_of = edge_left[0, 0]
    right_of = edge_right[0, 0]
    node_of = edge_node[0, 0]
    weight_of = edge_weight[0, 0]
    pick_weight = (weight_of[:, None] == jnp.arange(NW, dtype=jnp.int32)[None, :]).astype(
        jnp.float32
    )
    edge_coef = jnp.dot(pick_weight, weight_table, precision=high)
    member = (node_of[:, None] == jnp.arange(NODES, dtype=jnp.int32)[None, :]).astype(jnp.float32)
    gain_real = member * edge_coef[:, 0:1]
    gain_imag = member * edge_coef[:, 1:2]
    every_block = block_products(left_all, whole_peram)
    left_times = every_block[left_of]
    right_pick = right_all[right_of]
    prod_real = jnp.einsum(
        "eij,ejk->eik", left_times[:, 0], right_pick[:, 0], preferred_element_type=jnp.float32
    ) - jnp.einsum(
        "eij,ejk->eik", left_times[:, 1], right_pick[:, 1], preferred_element_type=jnp.float32
    )
    prod_imag = jnp.einsum(
        "eij,ejk->eik", left_times[:, 0], right_pick[:, 1], preferred_element_type=jnp.float32
    ) + jnp.einsum(
        "eij,ejk->eik", left_times[:, 1], right_pick[:, 0], preferred_element_type=jnp.float32
    )
    term_real = jnp.einsum("en,eik->ink", gain_real, prod_real, precision=high) - jnp.einsum(
        "en,eik->ink", gain_imag, prod_imag, precision=high
    )
    term_imag = jnp.einsum("en,eik->ink", gain_real, prod_imag, precision=high) + jnp.einsum(
        "en,eik->ink", gain_imag, prod_real, precision=high
    )
    node_share = lax.psum_scatter(
        jnp.stack([term_real, term_imag], 2), "snk", scatter_dimension=0, tiled=True
    )
    summed = lax.psum(node_share, "src")
    return summed.astype(jnp.bfloat16)


def solution(mesh):
    return jax.shard_map(
        shards,
        mesh=mesh,
        in_specs=(
            P("src", None, None, None, "snk"),
            P("snk", None, None, None, None),
            P("src", "snk", None),
            P("src", "snk", None),
            P("src", "snk", None),
            P("src", "snk", None),
            P(),
        ),
        out_specs=P("snk", None, None, None),
        check_vma=False,
    )
```

profile of v0, /device:TPU:1, one launch (start us, length us, event | category | flops | bytes accessed | tf_op | source)
XLA Modules:
  0.0 261.9 jit_solution(3890126083544399881)
XLA Ops:
  6.5 0.0 copy-start
  6.5 6.5 %all-to-all-start = ((bf16[1,8,2,256,32]{3,4,2,0,1:T(8,128)(2,1)}), bf16[1,8,2,256,32]{3,4,2,0,1:T(8,128)(2,1)S(1)}, u32[]{:S(2)}, u32[]{:S(2)}) async-start(bf16[1,8,2,256,32]{3,4,2,0,1:T(8,128)(2,1)} %bitcast.109), calls=%async_computation | async-start | bytes 524288 | tf_op jit(solution)/shard_map/all_to_all | solution.py:36
  13.0 0.0 all-reduce.3.cloned.1.call-start
  13.1 1.0 select_bitcast_fusion
  14.1 0.0 all-reduce.3.cloned.1.call-update
  14.1 0.0 reduce-scatter.5.cloned.1.call-start
  14.2 0.7 fusion.50
  14.9 0.7 fusion.51
  15.5 0.0 copy-done
  15.5 0.8 fusion.28
  16.4 1.3 fusion.56
  17.7 2.7 %all-to-all-done = bf16[1,8,2,256,32]{3,4,2,0,1:T(8,128)(2,1)S(1)} async-done(((bf16[1,8,2,256,32]{3,4,2,0,1:T(8,128)(2,1)}), bf16[1,8,2,256,32]{3,4,2,0,1:T(8,128)(2,1)S(1)}, u32[]{:S(2)}, u32[]{:S(2)}) %all-to-all-start) | async-done | bytes 262176 | tf_op jit(solution)/shard_map/all_to_all | solution.py:36
  20.4 0.3 fusion.59
  20.7 0.3 fusion.58
  21.1 0.3 fusion.27
  21.4 0.3 fusion.26
  21.8 0.1 pad_maximum_fusion.1
  21.9 5.1 %gather_fusion = bf16[32,2,256,256]{3,2,1,0:T(8,128)(2,1)} fusion(bf16[4,2,256,256]{3,2,1,0:T(8,128)(2,1)S(1)} %pad_maximum_fusion.1, s32[1024]{0:T(1024)S(1)} %pad_clamp_fusion.1), kind=kCustom, calls=%fused_computation | custom fusion | bytes 16777344 | tf_op jit(solution)/shard_map/gather | solution.py:52
  27.0 69.5 %all-reduce.3.cloned.1.call-done = bf16[4,2,256,256]{3,2,1,0:T(8,128)(2,1)} async-done(((bf16[4,2,256,256]{3,2,1,0:T(8,128)(2,1)}), bf16[4,2,256,256]{3,2,1,0:T(8,128)(2,1)}) %all-reduce.3.cloned.1.call-update) | async-done | bytes 1048592 | tf_op jit(solution)/shard_map/psum | solution.py:12
  96.4 6.6 %gather_fusion.1 = bf16[32,2,256,256]{3,2,1,0:T(8,128)(2,1)} fusion(bf16[4,2,256,256]{3,2,1,0:T(8,128)(2,1)} %all-reduce.3.cloned.1.call-done, s32[1024]{0:T(1024)S(1)} %pad_clamp_fusion), kind=kCustom, calls=%fused_computation.1 | custom fusion | bytes 16777344 | tf_op jit(solution)/shard_map/gather | solution.py:53
  103.1 0.0 copy-start.2
  103.1 0.0 copy-start.3
  103.1 9.1 %fusion.8 = f32[32,256,256]{2,1,0:T(8,128)} fusion(bf16[32,2,256,256]{3,2,1,0:T(8,128)(2,1)} %gather_fusion, bf16[32,2,256,256]{3,2,1,0:T(8,128)(2,1)} %gather_fusion.1), kind=kOutput, calls=%fused_computation.14 | convolution fusion | flops 1073741824 | bytes 16777216 | tf_op jit(solution)/shard_map/eij,ejk->eik/dot_general | solution.py:59
  112.2 0.0 copy-done.2
  112.2 2.1 copy-done.3
  114.3 4.5 %fusion.9 = f32[32,256,256]{2,1,0:T(8,128)} fusion(bf16[32,2,256,256]{3,2,1,0:T(8,128)(2,1)S(1)} %copy-done.2, bf16[32,2,256,256]{3,2,1,0:T(8,128)(2,1)S(1)} %copy-done.3), kind=kOutput, calls=%fused_computation.15 | convolution fusion | flops 1073741824 | bytes 16777216 | tf_op jit(solution)/shard_map/eij,ejk->eik/dot_general | solution.py:54
  118.8 0.0 copy-start.4
  118.8 5.9 %fusion.13 = f32[32,256,256]{2,1,0:T(8,128)S(1)} fusion(f32[32,256,256]{2,1,0:T(8,128)} %fusion.8, bf16[32,2,256,256]{3,2,1,0:T(8,128)(2,1)} %gather_fusion.1, bf16[32,2,256,256]{3,2,1,0:T(8,128)(2,1)S(1)} %copy-done.2), kind=kOutput, calls=%fused_computation.19 | convolution fusion | flops 1075838976 | bytes 25165824 | tf_op jit(solution)/shard_map/eij,ejk->eik/dot_general | solution.py:61
  124.8 0.0 copy-done.4
  124.8 9.3 %fusion = f32[256,256,4]{1,2,0:T(4,128)S(1)} fusion(f32[32,256,256]{2,1,0:T(8,128)S(1)} %fusion.13, f32[32]{0:T(128)S(1)} %get-tuple-element.10, s32[32]{0:T(128)S(1)} %bitcast.110), kind=kOutput, calls=%fused_computation.2 | convolution fusion | flops 100663552 | bytes 9437440 | tf_op jit(solution)/shard_map/en,eik->ink/dot_general | solution.py:67
  134.1 9.1 %fusion.2 = f32[256,256,4]{1,2,0:T(4,128)S(1)} fusion(f32[32,256,256]{2,1,0:T(8,128)S(1)} %fusion.13, f32[32]{0:T(128)S(1)} %get-tuple-element.9, s32[32]{0:T(128)S(1)} %bitcast.111), kind=kOutput, calls=%fused_computation.4 | convolution fusion | flops 100663552 | bytes 9437440 | tf_op jit(solution)/shard_map/en,eik->ink/dot_general | solution.py:64
  143.1 6.1 %fusion.12 = f32[32,256,256]{2,1,0:T(8,128)S(1)} fusion(f32[32,256,256]{2,1,0:T(8,128)} %fusion.9, bf16[32,2,256,256]{3,2,1,0:T(8,128)(2,1)} %gather_fusion.1, bf16[32,2,256,256]{3,2,1,0:T(8,128)(2,1)S(1)} %copy-done.2), kind=kOutput, calls=%fused_computation.18 | convolution fusion | flops 1075838976 | bytes 25165824 | tf_op jit(solution)/shard_map/eij,ejk->eik/dot_general | solution.py:56
  149.3 9.1 %fusion.23 = f32[256,4,1,256]{3,1,0,2:T(4,128)S(1)} fusion(f32[256,256,4]{1,2,0:T(4,128)S(1)} %fusion, f32[32,256,256]{2,1,0:T(8,128)S(1)} %fusion.12, f32[32]{0:T(128)S(1)} %get-tuple-element.9, s32[32]{0:T(128)S(1)} %bitcast.112), kind=kOutput, calls=%fused_computation.27 | convolution fusion | flops 100925696 | bytes 10486016 | tf_op jit(solution)/shard_map/en,eik->ink/dot_general | solution.py:67
  158.4 0.0 copy-start.1
  158.5 9.4 %fusion.17 = f32[256,4,1,256]{3,1,0,2:T(4,128)S(1)} fusion(f32[256,256,4]{1,2,0:T(4,128)S(1)} %fusion.2, f32[32,256,256]{2,1,0:T(8,128)S(1)} %fusion.12, f32[32]{0:T(128)S(1)} %get-tuple-element.10, s32[32]{0:T(128)S(1)} %bitcast.113), kind=kOutput, calls=%fused_computation.25 | convolution fusion | flops 100925696 | bytes 10486016 | tf_op jit(solution)/shard_map/en,eik->ink/dot_general | solution.py:64
  167.8 0.5 copy_bitcast_fusion
  168.3 2.1 reshape.81
  170.5 0.0 reduce-scatter.5.cloned.1.call-update
  170.5 66.5 %reduce-scatter.5.cloned.1.call-done = f32[32,2048]{1,0:T(8,128)} async-done(((f32[256,2048]{1,0:T(8,128)}), f32[32,2048]{1,0:T(8,128)}) %reduce-scatter.5.cloned.1.call-update) | async-done | bytes 262160
  237.0 1.1 reshape.82
  238.1 15.7 %all-reduce.4 = bf16[32,4,2,256]{3,1,0,2:T(4,128)(2,1)S(1)} all-reduce(f32[32,4,2,256]{3,1,0,2:T(4,128)S(1)} %copy.37), channel_id=1, replica_groups=mesh['src'=4,'snk'=8] {'src'}, use_global_device_ids=true, to_apply=%region_2.3 | all-reduce | flops 65536 | bytes 393216 | tf_op jit(solution)/shard_map/psum | solution.py:73
  253.8 0.8 copy.35
  254.6 0.0 copy-done.1
  (5 shorter events, 0.1 us)
Async XLA Ops:
  6.5 9.0 %copy-start = (f32[16,2]{0,1:T(2,128)S(1)}, f32[16,2]{0,1:T(2,128)}, u32[]{:S(2)}) copy-start(f32[16,2]{0,1:T(2,128)} %param.13) | copy-start | bytes 388
  6.5 13.8 %all-to-all-start = ((bf16[1,8,2,256,32]{3,4,2,0,1:T(8,128)(2,1)}), bf16[1,8,2,256,32]{3,4,2,0,1:T(8,128)(2,1)S(1)}, u32[]{:S(2)}, u32[]{:S(2)}) async-start(bf16[1,8,2,256,32]{3,4,2,0,1:T(8,128)(2,1)} %bitcast.109), calls=%async_computation | async-start | bytes 524288 | tf_op jit(solution)/shard_map/all_to_all | solution.py:36
  13.0 83.4 %all-reduce.3.cloned.1.call-start = ((), (), s32[]{:S(2)}) async-start(), calls=%async_computation.2 | async-start | bytes 2097152 | tf_op jit(solution)/shard_map/psum | solution.py:12
  14.1 222.8 %reduce-scatter.5.cloned.1.call-start = ((), (), s32[]{:S(2)}) async-start(), calls=%async_computation.3 | async-start | bytes 2359296
  103.1 9.1 %copy-start.2 = (bf16[32,2,256,256]{3,2,1,0:T(8,128)(2,1)S(1)}, bf16[32,2,256,256]{3,2,1,0:T(8,128)(2,1)}, u32[]{:S(2)}) copy-start(bf16[32,2,256,256]{3,2,1,0:T(8,128)(2,1)} %gather_fusion) | copy-start | bytes 25165828
  103.1 11.2 %copy-start.3 = (bf16[32,2,256,256]{3,2,1,0:T(8,128)(2,1)S(1)}, bf16[32,2,256,256]{3,2,1,0:T(8,128)(2,1)}, u32[]{:S(2)}) copy-start(bf16[32,2,256,256]{3,2,1,0:T(8,128)(2,1)} %gather_fusion.1) | copy-start | bytes 25165828
  118.8 5.9 %copy-start.4 = (s32[1,1,32]{2,1,0:T(1,128)S(1)}, s32[1,1,32]{2,1,0:T(1,128)}, u32[]{:S(2)}) copy-start(s32[1,1,32]{2,1,0:T(1,128)} %param.11) | copy-start | bytes 388
  158.4 96.1 %copy-start.1 = (f32[16,2]{0,1:T(2,128)S(1)}, f32[16,2]{0,1:T(2,128)}, u32[]{:S(2)}) copy-start(f32[16,2]{0,1:T(2,128)} %param.13) | copy-start | bytes 388
Sparse Core Ops, SparseCore 0:
  17.4 79.0 all-reduce.2
  170.6 66.2 reduce-scatter.4
where the time goes:
time: 265 us; the launch traced here: 262 us
  waiting for transfers between devices  139 us (52%)
  matrix products  64.7 us (24%)
  local copies, waits for them, and re-layouts  19.3 us (7%)
  blocking collectives  15.7 us (6%)
  between operations  14 us (5%)
  starting transfers between devices  6.56 us (2%)
  other arithmetic  2.94 us (1%)
    psum x1, waiting for transfers between devices, from_root(): return lax.psum(kept, axis)  69.5 us
    unnamed x3, waiting for transfers between devices  66.5 us
    psum x1, blocking collectives, shards(): summed = lax.psum(node_share, 'src')  15.7 us
    dot_general x1, matrix products, shards(): jnp.einsum('en,eik->ink', gain_real, prod_real, precision=high)  9.39 us
    dot_general x1, matrix products, shards(): jnp.einsum('en,eik->ink', gain_real, prod_imag, precision=high)  9.26 us
    dot_general x1, matrix products, shards(): jnp.einsum('en,eik->ink', gain_imag, prod_real, precision=high)  9.13 us
    dot_general x1, matrix products, shards(): jnp.einsum('eij,ejk->eik', left_times[:, 0], right_pick[:, 1], preferred_...  9.13 us
    dot_general x1, matrix products, shards(): jnp.einsum('en,eik->ink', gain_imag, prod_imag, precision=high)  9.08 us
  transfers between devices with their start and end apart: 3, of which 3 were waited for; matrix products, arithmetic and copies ran while one was open for 4% of the time, Pallas kernels for 0%

commit v1 on v0

v1 whole, which is shorter than its diff:
```python
import functools

import jax
import jax.numpy as jnp
from jax import lax
from jax.experimental import pallas as pl
from jax.experimental.pallas import tpu as pltpu
from jax.sharding import PartitionSpec as P

NODES = 4
NW = 16
MESH = pl.DeviceIdType.MESH
F32 = jnp.float32
BF16 = jnp.bfloat16
MIX_ROWS = 16


def kernel(
    n_src, n_snk, mom, order,
    tau_ref, blocks_ref, left_ref, right_ref, node_ref, weight_ref, table_ref,
    out_ref,
    tau_in, right_buf, coef, mixed, tau_cat, prod, part, part_in, share, share_in, done,
    tau_send, tau_recv, cast_send, cast_recv, part_send, part_recv, share_send, share_recv, done_send, done_recv,
):
    s = lax.axis_index("src")
    t = lax.axis_index("snk")
    planes = NODES * 2 // n_src
    rows = order // n_snk
    half = mom
    root = s * (n_snk // n_src)
    high, low = t // 2, t % 2
    root_high, root_low = root // 2, root % 2
    other = 1 - low
    is_root = t == root
    pair_is_root = (high == root_high) & (other == root_low)
    goes_up = (high >= root_high) & (high + 1 < n_snk // 2)
    goes_down = (high <= root_high) & (high >= 1)

    def snk_peer(d):
        return lax.rem(t + d, n_snk)

    def src_peer(d):
        return lax.rem(s + d, n_src)

    barrier = pltpu.get_barrier_semaphore()
    for d in range(1, n_snk):
        pl.semaphore_signal(barrier, inc=1, device_id=(s, snk_peer(d)), device_id_type=MESH)
    for d in range(1, n_src):
        pl.semaphore_signal(barrier, inc=1, device_id=(src_peer(d), t), device_id_type=MESH)
    pl.semaphore_wait(barrier, n_snk + n_src - 2)

    def cast(piece, kind, q, target):
        return pltpu.make_async_remote_copy(
            src_ref=right_buf.at[piece], dst_ref=right_buf.at[piece],
            send_sem=cast_send.at[kind, q], recv_sem=cast_recv.at[piece],
            device_id=(s, target), device_id_type=MESH,
        )

    def cast_ways(q):
        mine = low * half + q
        return (
            (goes_up, cast(mine, 0, q, jnp.minimum(t + 2, n_snk - 1))),
            (goes_down, cast(mine, 1, q, jnp.maximum(t - 2, 0))),
            (jnp.logical_not(pair_is_root), cast(mine, 2, q, high * 2 + other)),
        )

    def cast_rest(q):
        return cast(other * half + q, 3, q, high * 2 + other)

    def cast_arrived(piece):
        @pl.when(jnp.logical_not(is_root))
        def _():
            cast(piece, 0, 0, high * 2 + other).wait_recv()

    @pl.when(is_root)
    def _():
        for piece in range(2 * mom):
            right_buf[piece] = blocks_ref[piece]
        for q in range(half):
            cast_rest(q).start()

    tau_copies = []
    for d in range(1, n_snk):
        copy = pltpu.make_async_remote_copy(
            src_ref=tau_ref.at[snk_peer(d)], dst_ref=tau_in.at[t],
            send_sem=tau_send.at[d - 1], recv_sem=tau_recv.at[d - 1],
            device_id=(s, snk_peer(d)), device_id_type=MESH,
        )
        copy.start()
        tau_copies.append(copy)
    tau_in[t] = tau_ref[t]

    table_row = lax.broadcasted_iota(jnp.int32, (NW, 1), 0)
    picks = table_row == weight_ref[...]
    slot = (node_ref[...] * mom + right_ref[...]) * mom + left_ref[...]
    slots = NODES * mom * mom
    feeds = lax.broadcasted_iota(jnp.int32, (slots, 1), 0) == slot
    for c in range(2):
        gain = jnp.sum(jnp.where(picks, table_ref[:, c : c + 1], 0.0), axis=0, keepdims=True)
        total = jnp.sum(jnp.where(feeds, gain, 0.0), axis=1, keepdims=True)
        coef[c] = jnp.broadcast_to(total, (slots, order))

    def mix_node(n):
        def step(i, carry):
            span = pl.ds(pl.multiple_of(i * MIX_ROWS, MIX_ROWS), MIX_ROWS)
            real = [blocks_ref[2 * a, span, :].astype(F32) for a in range(mom)]
            imag = [blocks_ref[2 * a + 1, span, :].astype(F32) for a in range(mom)]
            for b in range(mom):
                sum_real = sum_imag = 0.0
                for a in range(mom):
                    k = (n * mom + b) * mom + a
                    gain_real, gain_imag = coef[0, k : k + 1, :], coef[1, k : k + 1, :]
                    sum_real += gain_real * real[a] - gain_imag * imag[a]
                    sum_imag += gain_real * imag[a] + gain_imag * real[a]
                at = 2 * b * order
                mixed[n, span, at : at + order] = sum_real.astype(BF16)
                mixed[n, span, at + order : at + 2 * order] = sum_imag.astype(BF16)
            return carry

        lax.fori_loop(0, order // MIX_ROWS, step, 0)

    with jax.named_scope("relay_and_mix"):
        for q in range(max(half, NODES)):
            if q < half:
                cast_arrived(low * half + q)
                for taken, copy in cast_ways(q):
                    pl.when(taken)(copy.start)
            if q < NODES:
                mix_node(q)

    with jax.named_scope("tau"):
        for copy in tau_copies:
            copy.wait_recv()
        whole = tau_in[...].astype(F32)
        tau_real = whole[:, 0].reshape(order, order).T
        tau_imag = whole[:, 1].reshape(order, order).T
        tau_cat[:order, :order] = tau_real.astype(BF16)
        tau_cat[:order, order:] = (-tau_imag).astype(BF16)
        tau_cat[order:, :order] = tau_imag.astype(BF16)
        tau_cat[order:, order:] = tau_real.astype(BF16)

    with jax.named_scope("times_right"):
        for j in range(mom):
            if 2 * j < mom:
                b = low * (mom // 2) + j
            else:
                b = other * (mom // 2) + j - mom // 2
                cast_arrived(2 * b)
                cast_arrived(2 * b + 1)
            right = right_buf[pl.ds(2 * b, 2)].reshape(2 * order, order)
            both = jnp.dot(tau_cat[...], right, preferred_element_type=F32)
            prod[0, b, :order] = both[:order].astype(BF16)
            prod[0, b, order:] = (-both[order:]).astype(BF16)
            prod[1, b, :order] = both[order:].astype(BF16)
            prod[1, b, order:] = both[:order].astype(BF16)

    def plane_of(p):
        return jnp.dot(
            mixed[p // 2], prod[p % 2].reshape(2 * mom * order, order), preferred_element_type=F32
        )

    part_copies = []
    with jax.named_scope("nodes"):
        for d in range(1, n_src):
            for q in range(planes):
                part[d - 1, q] = plane_of(src_peer(d) * planes + q).astype(BF16)
            copy = pltpu.make_async_remote_copy(
                src_ref=part.at[d - 1], dst_ref=part_in.at[d - 1],
                send_sem=part_send.at[d - 1], recv_sem=part_recv.at[d - 1],
                device_id=(src_peer(d), t), device_id_type=MESH,
            )
            copy.start()
            part_copies.append(copy)
        own = [plane_of(s * planes + q) for q in range(planes)]

    with jax.named_scope("sum_src"):
        for copy in part_copies:
            copy.wait_recv()
        for q in range(planes):
            total = own[q]
            for d in range(1, n_src):
                total += part_in[d - 1, q].astype(F32)
            for k in range(n_snk):
                share[k, q] = total[k * rows : (k + 1) * rows].astype(BF16)

    with jax.named_scope("sum_snk"):
        share_copies = []
        for d in range(1, n_snk):
            copy = pltpu.make_async_remote_copy(
                src_ref=share.at[snk_peer(d)], dst_ref=share_in.at[d - 1],
                send_sem=share_send.at[d - 1], recv_sem=share_recv.at[d - 1],
                device_id=(s, snk_peer(d)), device_id_type=MESH,
            )
            copy.start()
            share_copies.append(copy)
        total = share[t].astype(F32)
        for d in range(1, n_snk):
            share_copies[d - 1].wait_recv()
            total += share_in[d - 1].astype(F32)
        done[s] = total.astype(BF16)

    with jax.named_scope("spread"):
        done_copies = []
        for d in range(1, n_src):
            copy = pltpu.make_async_remote_copy(
                src_ref=done.at[s], dst_ref=done.at[s],
                send_sem=done_send.at[d - 1], recv_sem=done_recv.at[d - 1],
                device_id=(src_peer(d), t), device_id_type=MESH,
            )
            copy.start()
            done_copies.append(copy)
        for copy in done_copies:
            copy.wait_recv()
        out_ref[...] = done[...]

    for q in range(half):
        for taken, copy in cast_ways(q):
            pl.when(taken)(copy.wait_send)
        pl.when(is_root)(cast_rest(q).wait_send)
    for copy in tau_copies + part_copies + share_copies + done_copies:
        copy.wait_send()


def shards(peram, meson_blocks, edge_left, edge_right, edge_node, edge_weight, weight_table):
    n_src, n_snk = lax.axis_size("src"), lax.axis_size("snk")
    mom, order = meson_blocks.shape[1], meson_blocks.shape[3]
    rows, planes = order // n_snk, NODES * 2 // n_src
    tau = jnp.swapaxes(peram[0], 2, 3)
    blocks = meson_blocks.reshape(2 * mom, order, order)
    edges = [e.reshape(1, -1) for e in (edge_left, edge_right, edge_node, edge_weight)]
    dma = pltpu.SemaphoreType.DMA
    out = pl.pallas_call(
        functools.partial(kernel, n_src, n_snk, mom, order),
        out_shape=jax.ShapeDtypeStruct((n_src, planes, rows, order), BF16),
        in_specs=[pl.BlockSpec(memory_space=pltpu.VMEM)] * 7,
        out_specs=pl.BlockSpec(memory_space=pltpu.VMEM),
        scratch_shapes=[
            pltpu.VMEM((n_snk, 2, rows, order), BF16),
            pltpu.VMEM((2 * mom, order, order), BF16),
            pltpu.VMEM((2, NODES * mom * mom, order), F32),
            pltpu.VMEM((NODES, order, 2 * mom * order), BF16),
            pltpu.VMEM((2 * order, 2 * order), BF16),
            pltpu.VMEM((2, mom, 2 * order, order), BF16),
            pltpu.VMEM((n_src - 1, planes, order, order), BF16),
            pltpu.VMEM((n_src - 1, planes, order, order), BF16),
            pltpu.VMEM((n_snk, planes, rows, order), BF16),
            pltpu.VMEM((n_snk - 1, planes, rows, order), BF16),
            pltpu.VMEM((n_src, planes, rows, order), BF16),
            dma((n_snk - 1,)), dma((n_snk - 1,)),
            dma((4, mom)), dma((2 * mom,)),
            dma((n_src - 1,)), dma((n_src - 1,)),
            dma((n_snk - 1,)), dma((n_snk - 1,)),
            dma((n_src - 1,)), dma((n_src - 1,)),
        ],
        compiler_params=pltpu.CompilerParams(
            collective_id=0, has_side_effects=True, vmem_limit_bytes=40 * 2**20
        ),
    )(tau, blocks, *edges, weight_table)
    out = out.reshape(NODES, 2, rows, order)
    return jnp.transpose(out, (2, 0, 1, 3))


def solution(mesh):
    return jax.shard_map(
        shards,
        mesh=mesh,
        in_specs=(
            P("src", None, None, None, "snk"),
            P("snk", None, None, None, None),
            P("src", "snk", None),
            P("src", "snk", None),
            P("src", "snk", None),
            P("src", "snk", None),
            P(),
        ),
        out_specs=P("snk", None, None, None),
        check_vma=False,
    )
```

time: 265 us -> 57.1 us (0.22)
  the two profiles are of different devices: /device:TPU:1 before, /device:TPU:29 now
where the time goes in v1:
time: 57.1 us; the launch traced here: 56.6 us
  Pallas kernels  52.2 us (91%)
  local copies, waits for them, and re-layouts  4.34 us (8%)
    pallas_call x1, Pallas kernels, shards(): pl.pallas_call(functools.partial(kernel, n_src, n_snk, mom, order), out_s...  52.2 us
    unnamed x15, local copies, waits for them, and re-layouts  3.55 us

profile of v1, /device:TPU:29, one launch (start us, length us, event | category | flops | bytes accessed | tf_op | source)
XLA Modules:
  0.0 56.6 jit_solution(15132216341762697157)
XLA Ops:
  0.0 0.0 copy-start.6
  0.0 0.7 %copy-done.6 = f32[16,2]{0,1:T(2,128)S(1)} copy-done((f32[16,2]{0,1:T(2,128)S(1)}, f32[16,2]{0,1:T(2,128)}, u32[]{:S(2)}) %copy-start.6) | copy-done | bytes 152
  0.7 0.0 copy-start.2
  0.7 0.0 copy-start.3
  0.7 0.0 copy-start.4
  0.7 0.0 copy-start.5
  0.7 0.1 copy.8.table_ref
  0.8 0.6 copy-done.2
  1.3 0.0 copy-done.3
  1.4 0.0 copy-done.4
  1.4 0.0 copy-done.5
  1.4 0.0 copy-start
  1.4 1.2 %copy-done = bf16[1,4,2,256,256]{4,3,2,1,0:T(8,128)(2,1)S(1)} copy-done((bf16[1,4,2,256,256]{4,3,2,1,0:T(8,128)(2,1)S(1)}, bf16[1,4,2,256,256]{4,3,2,1,0:T(8,128)(2,1)}, u32[]{:S(2)}) %copy-start) | copy-done | bytes 1048600
  2.6 0.0 copy-start.1
  2.6 0.9 %copy-done.1 = bf16[1,8,2,256,32]{3,4,2,1,0:T(8,128)(2,1)S(1)} copy-done((bf16[1,8,2,256,32]{3,4,2,1,0:T(8,128)(2,1)S(1)}, bf16[1,8,2,256,32]{3,4,2,1,0:T(8,128)(2,1)}, u32[]{:S(2)}) %copy-start.1) | copy-done | bytes 262168
  3.6 52.2 %shard_map.73 = bf16[4,2,32,256]{3,2,1,0:T(8,128)(2,1)S(1)} custom-call(bf16[8,2,32,256]{3,2,1,0:T(8,128)(2,1)S(1)} %bitcast.11, bf16[8,256,256]{2,1,0:T(8,128)(2,1)S(1)} %bitcast.9, s32[1,32]{1,0:T(1,128)S(1)} %bitcast.12, s32[1,32]{1,0:T(1,128)S(1)} %bitcast.13, s32[1,32]{1,0:T(1,128)S(1)} %bitcast.14, s32[1,32]{1,0:T(1,128)S(1)} %bitcast.15, ...), custom_call_target="tpu_custom_call" | custom-call | tf_op jit(solution)/shard_map/pallas_call | solution.py:232
  55.8 0.8 %copy.9 = bf16[32,4,2,256]{3,2,1,0:T(2,128)(2,1)} copy(bf16[32,4,2,256]{3,0,2,1:T(8,128)(2,1)S(1)} %bitcast.10) | data formatting | bytes 262144 | tf_op jit(solution)/shard_map/transpose | solution.py:260
Async XLA Ops:
  0.0 0.7 %copy-start.6 = (f32[16,2]{0,1:T(2,128)S(1)}, f32[16,2]{0,1:T(2,128)}, u32[]{:S(2)}) copy-start(f32[16,2]{0,1:T(2,128)} %param.13) | copy-start | bytes 388
  0.7 0.7 %copy-start.2 = (s32[1,1,32]{2,1,0:T(1,128)S(1)}, s32[1,1,32]{2,1,0:T(1,128)}, u32[]{:S(2)}) copy-start(s32[1,1,32]{2,1,0:T(1,128)} %param.9) | copy-start | bytes 388
  0.7 0.7 %copy-start.3 = (s32[1,1,32]{2,1,0:T(1,128)S(1)}, s32[1,1,32]{2,1,0:T(1,128)}, u32[]{:S(2)}) copy-start(s32[1,1,32]{2,1,0:T(1,128)} %param.10) | copy-start | bytes 388
  0.7 0.7 %copy-start.4 = (s32[1,1,32]{2,1,0:T(1,128)S(1)}, s32[1,1,32]{2,1,0:T(1,128)}, u32[]{:S(2)}) copy-start(s32[1,1,32]{2,1,0:T(1,128)} %param.11) | copy-start | bytes 388
  0.7 0.7 %copy-start.5 = (s32[1,1,32]{2,1,0:T(1,128)S(1)}, s32[1,1,32]{2,1,0:T(1,128)}, u32[]{:S(2)}) copy-start(s32[1,1,32]{2,1,0:T(1,128)} %param.12) | copy-start | bytes 388
  1.4 1.2 %copy-start = (bf16[1,4,2,256,256]{4,3,2,1,0:T(8,128)(2,1)S(1)}, bf16[1,4,2,256,256]{4,3,2,1,0:T(8,128)(2,1)}, u32[]{:S(2)}) copy-start(bf16[1,4,2,256,256]{4,3,2,1,0:T(8,128)(2,1)} %param.8) | copy-start | bytes 3145732
  2.6 0.9 %copy-start.1 = (bf16[1,8,2,256,32]{3,4,2,1,0:T(8,128)(2,1)S(1)}, bf16[1,8,2,256,32]{3,4,2,1,0:T(8,128)(2,1)}, u32[]{:S(2)}) copy-start(bf16[1,8,2,256,32]{3,4,2,1,0:T(8,128)(2,1)} %param.7) | copy-start | bytes 786436

commit v2 on v1

--- a/solution.py
+++ b/solution.py
@@ -13,6 +13,7 @@
 F32 = jnp.float32
 BF16 = jnp.bfloat16
 MIX_ROWS = 16
+SPLIT = 4
 
 
 def kernel(
@@ -26,7 +27,8 @@
     t = lax.axis_index("snk")
     planes = NODES * 2 // n_src
     rows = order // n_snk
-    half = mom
+    half = mom * SPLIT
+    cut = order // SPLIT
     root = s * (n_snk // n_src)
     high, low = t // 2, t % 2
     root_high, root_low = root // 2, root % 2
@@ -68,16 +70,21 @@
         return cast(other * half + q, 3, q, high * 2 + other)
 
     def cast_arrived(piece):
-        @pl.when(jnp.logical_not(is_root))
-        def _():
-            cast(piece, 0, 0, high * 2 + other).wait_recv()
+        cast(piece, 0, 0, high * 2 + other).wait_recv()
 
     @pl.when(is_root)
     def _():
-        for piece in range(2 * mom):
-            right_buf[piece] = blocks_ref[piece]
-        for q in range(half):
+        for block in range(2 * mom):
+            for r in range(SPLIT):
+                right_buf[block * SPLIT + r] = blocks_ref[block, r * cut : (r + 1) * cut]
+
+        def send(q, carry):
             cast_rest(q).start()
+            for taken, copy in cast_ways(q):
+                pl.when(taken)(copy.start)
+            return carry
+
+        lax.fori_loop(0, half, send, 0)
 
     tau_copies = []
     for d in range(1, n_snk):
@@ -100,7 +107,7 @@
         total = jnp.sum(jnp.where(feeds, gain, 0.0), axis=1, keepdims=True)
         coef[c] = jnp.broadcast_to(total, (slots, order))
 
-    def mix_node(n):
+    def mix_node(n, first, last):
         def step(i, carry):
             span = pl.ds(pl.multiple_of(i * MIX_ROWS, MIX_ROWS), MIX_ROWS)
             real = [blocks_ref[2 * a, span, :].astype(F32) for a in range(mom)]
@@ -117,16 +124,26 @@
                 mixed[n, span, at + order : at + 2 * order] = sum_imag.astype(BF16)
             return carry
 
-        lax.fori_loop(0, order // MIX_ROWS, step, 0)
-
+        lax.fori_loop(first, last, step, 0)
+
+    turns = half // NODES
+    mix_steps = order // MIX_ROWS // turns
     with jax.named_scope("relay_and_mix"):
-        for q in range(max(half, NODES)):
-            if q < half:
-                cast_arrived(low * half + q)
-                for taken, copy in cast_ways(q):
-                    pl.when(taken)(copy.start)
-            if q < NODES:
-                mix_node(q)
+        for n in range(NODES):
+
+            def relay(j, carry):
+                q = n * turns + j
+
+                @pl.when(jnp.logical_not(is_root))
+                def _():
+                    cast_arrived(low * half + q)
+                    for taken, copy in cast_ways(q):
+                        pl.when(taken)(copy.start)
+
+                mix_node(n, j * mix_steps, (j + 1) * mix_steps)
+                return carry
+
+            lax.fori_loop(0, turns, relay, 0)
 
     with jax.named_scope("tau"):
         for copy in tau_copies:
@@ -145,9 +162,12 @@
                 b = low * (mom // 2) + j
             else:
                 b = other * (mom // 2) + j - mom // 2
-                cast_arrived(2 * b)
-                cast_arrived(2 * b + 1)
-            right = right_buf[pl.ds(2 * b, 2)].reshape(2 * order, order)
+                @pl.when(jnp.logical_not(is_root))
+                def _():
+                    for r in range(2 * SPLIT):
+                        cast_arrived(2 * b * SPLIT + r)
+
+            right = right_buf[pl.ds(2 * b * SPLIT, 2 * SPLIT)].reshape(2 * order, order)
             both = jnp.dot(tau_cat[...], right, preferred_element_type=F32)
             prod[0, b, :order] = both[:order].astype(BF16)
             prod[0, b, order:] = (-both[order:]).astype(BF16)
@@ -213,10 +233,13 @@
             copy.wait_recv()
         out_ref[...] = done[...]
 
-    for q in range(half):
+    def sent(q, carry):
         for taken, copy in cast_ways(q):
             pl.when(taken)(copy.wait_send)
         pl.when(is_root)(cast_rest(q).wait_send)
+        return carry
+
+    lax.fori_loop(0, half, sent, 0)
     for copy in tau_copies + part_copies + share_copies + done_copies:
         copy.wait_send()
 
@@ -236,7 +259,7 @@
         out_specs=pl.BlockSpec(memory_space=pltpu.VMEM),
         scratch_shapes=[
             pltpu.VMEM((n_snk, 2, rows, order), BF16),
-            pltpu.VMEM((2 * mom, order, order), BF16),
+            pltpu.VMEM((2 * mom * SPLIT, order // SPLIT, order), BF16),
             pltpu.VMEM((2, NODES * mom * mom, order), F32),
             pltpu.VMEM((NODES, order, 2 * mom * order), BF16),
             pltpu.VMEM((2 * order, 2 * order), BF16),
@@ -247,7 +270,7 @@
             pltpu.VMEM((n_snk - 1, planes, rows, order), BF16),
             pltpu.VMEM((n_src, planes, rows, order), BF16),
             dma((n_snk - 1,)), dma((n_snk - 1,)),
-            dma((4, mom)), dma((2 * mom,)),
+            dma((4, mom * SPLIT)), dma((2 * mom * SPLIT,)),
             dma((n_src - 1,)), dma((n_src - 1,)),
             dma((n_snk - 1,)), dma((n_snk - 1,)),
             dma((n_src - 1,)), dma((n_src - 1,)),

time: 57.1 us -> 60.2 us (1.054)
  Pallas kernels: 52.2 us -> 54.7 us
    pallas_call x1, Pallas kernels: 52.2 us -> 54.7 us  [shards(): pl.pallas_call(functools.partial(kernel, n_src, n_snk, mom, order), out_s...]
where the time goes in v2:
time: 60.2 us; the launch traced here: 59.1 us
  Pallas kernels  54.7 us (91%)
  local copies, waits for them, and re-layouts  4.34 us (7%)
    pallas_call x1, Pallas kernels, shards(): pl.pallas_call(functools.partial(kernel, n_src, n_snk, mom, order), out_s...  54.7 us
    unnamed x15, local copies, waits for them, and re-layouts  3.55 us

profile of v2, /device:TPU:29, one launch (start us, length us, event | category | flops | bytes accessed | tf_op | source)
XLA Modules:
  0.0 59.1 jit_solution(667424036757465964)
XLA Ops:
  0.0 0.0 copy-start.6
  0.0 0.7 %copy-done.6 = f32[16,2]{0,1:T(2,128)S(1)} copy-done((f32[16,2]{0,1:T(2,128)S(1)}, f32[16,2]{0,1:T(2,128)}, u32[]{:S(2)}) %copy-start.6) | copy-done | bytes 152
  0.7 0.0 copy-start.2
  0.7 0.0 copy-start.3
  0.7 0.0 copy-start.4
  0.7 0.0 copy-start.5
  0.7 0.1 copy.8.table_ref
  0.8 0.6 copy-done.2
  1.3 0.0 copy-done.3
  1.4 0.0 copy-done.4
  1.4 0.0 copy-done.5
  1.4 0.0 copy-start
  1.4 1.2 %copy-done = bf16[1,4,2,256,256]{4,3,2,1,0:T(8,128)(2,1)S(1)} copy-done((bf16[1,4,2,256,256]{4,3,2,1,0:T(8,128)(2,1)S(1)}, bf16[1,4,2,256,256]{4,3,2,1,0:T(8,128)(2,1)}, u32[]{:S(2)}) %copy-start) | copy-done | bytes 1048600
  2.6 0.0 copy-start.1
  2.6 0.9 %copy-done.1 = bf16[1,8,2,256,32]{3,4,2,1,0:T(8,128)(2,1)S(1)} copy-done((bf16[1,8,2,256,32]{3,4,2,1,0:T(8,128)(2,1)S(1)}, bf16[1,8,2,256,32]{3,4,2,1,0:T(8,128)(2,1)}, u32[]{:S(2)}) %copy-start.1) | copy-done | bytes 262168
  3.6 54.7 %shard_map.73 = bf16[4,2,32,256]{3,2,1,0:T(8,128)(2,1)S(1)} custom-call(bf16[8,2,32,256]{3,2,1,0:T(8,128)(2,1)S(1)} %bitcast.11, bf16[8,256,256]{2,1,0:T(8,128)(2,1)S(1)} %bitcast.9, s32[1,32]{1,0:T(1,128)S(1)} %bitcast.12, s32[1,32]{1,0:T(1,128)S(1)} %bitcast.13, s32[1,32]{1,0:T(1,128)S(1)} %bitcast.14, s32[1,32]{1,0:T(1,128)S(1)} %bitcast.15, ...), custom_call_target="tpu_custom_call" | custom-call | tf_op jit(solution)/shard_map/pallas_call | solution.py:255
  58.3 0.8 %copy.9 = bf16[32,4,2,256]{3,2,1,0:T(2,128)(2,1)} copy(bf16[32,4,2,256]{3,0,2,1:T(8,128)(2,1)S(1)} %bitcast.10) | data formatting | bytes 262144 | tf_op jit(solution)/shard_map/transpose | solution.py:283
Async XLA Ops:
  0.0 0.7 %copy-start.6 = (f32[16,2]{0,1:T(2,128)S(1)}, f32[16,2]{0,1:T(2,128)}, u32[]{:S(2)}) copy-start(f32[16,2]{0,1:T(2,128)} %param.13) | copy-start | bytes 388
  0.7 0.7 %copy-start.2 = (s32[1,1,32]{2,1,0:T(1,128)S(1)}, s32[1,1,32]{2,1,0:T(1,128)}, u32[]{:S(2)}) copy-start(s32[1,1,32]{2,1,0:T(1,128)} %param.9) | copy-start | bytes 388
  0.7 0.7 %copy-start.3 = (s32[1,1,32]{2,1,0:T(1,128)S(1)}, s32[1,1,32]{2,1,0:T(1,128)}, u32[]{:S(2)}) copy-start(s32[1,1,32]{2,1,0:T(1,128)} %param.10) | copy-start | bytes 388
  0.7 0.7 %copy-start.4 = (s32[1,1,32]{2,1,0:T(1,128)S(1)}, s32[1,1,32]{2,1,0:T(1,128)}, u32[]{:S(2)}) copy-start(s32[1,1,32]{2,1,0:T(1,128)} %param.11) | copy-start | bytes 388
  0.7 0.7 %copy-start.5 = (s32[1,1,32]{2,1,0:T(1,128)S(1)}, s32[1,1,32]{2,1,0:T(1,128)}, u32[]{:S(2)}) copy-start(s32[1,1,32]{2,1,0:T(1,128)} %param.12) | copy-start | bytes 388
  1.4 1.2 %copy-start = (bf16[1,4,2,256,256]{4,3,2,1,0:T(8,128)(2,1)S(1)}, bf16[1,4,2,256,256]{4,3,2,1,0:T(8,128)(2,1)}, u32[]{:S(2)}) copy-start(bf16[1,4,2,256,256]{4,3,2,1,0:T(8,128)(2,1)} %param.8) | copy-start | bytes 3145732
  2.6 0.9 %copy-start.1 = (bf16[1,8,2,256,32]{3,4,2,1,0:T(8,128)(2,1)S(1)}, bf16[1,8,2,256,32]{3,4,2,1,0:T(8,128)(2,1)}, u32[]{:S(2)}) copy-start(bf16[1,8,2,256,32]{3,4,2,1,0:T(8,128)(2,1)} %param.7) | copy-start | bytes 786436

commit v3 on v1

--- a/solution.py
+++ b/solution.py
@@ -17,10 +17,10 @@
 
 def kernel(
     n_src, n_snk, mom, order,
-    tau_ref, blocks_ref, left_ref, right_ref, node_ref, weight_ref, table_ref,
+    tau_ref, blocks_hbm, left_ref, right_ref, node_ref, weight_ref, table_ref,
     out_ref,
-    tau_in, right_buf, coef, mixed, tau_cat, prod, part, part_in, share, share_in, done,
-    tau_send, tau_recv, cast_send, cast_recv, part_send, part_recv, share_send, share_recv, done_send, done_recv,
+    blocks_ref, tau_in, right_buf, coef, mixed, tau_cat, prod, part, part_in, share, share_in, done,
+    tau_send, tau_recv, cast_send, cast_recv, part_send, part_recv, share_send, share_recv, done_send, done_recv, local_sem,
 ):
     s = lax.axis_index("src")
     t = lax.axis_index("snk")
@@ -42,6 +42,13 @@
     def src_peer(d):
         return lax.rem(s + d, n_src)
 
+    load_blocks = pltpu.make_async_copy(blocks_hbm, blocks_ref, local_sem.at[0])
+    load_tau = pltpu.make_async_copy(tau_ref.at[t], tau_in.at[t], local_sem.at[1])
+    load_right = pltpu.make_async_copy(blocks_hbm, right_buf, local_sem.at[2])
+    pl.when(is_root)(load_right.start)
+    load_blocks.start()
+    load_tau.start()
+
     barrier = pltpu.get_barrier_semaphore()
     for d in range(1, n_snk):
         pl.semaphore_signal(barrier, inc=1, device_id=(s, snk_peer(d)), device_id_type=MESH)
@@ -74,8 +81,7 @@
 
     @pl.when(is_root)
     def _():
-        for piece in range(2 * mom):
-            right_buf[piece] = blocks_ref[piece]
+        load_right.wait()
         for q in range(half):
             cast_rest(q).start()
 
@@ -88,7 +94,6 @@
         )
         copy.start()
         tau_copies.append(copy)
-    tau_in[t] = tau_ref[t]
 
     table_row = lax.broadcasted_iota(jnp.int32, (NW, 1), 0)
     picks = table_row == weight_ref[...]
@@ -119,6 +124,7 @@
 
         lax.fori_loop(0, order // MIX_ROWS, step, 0)
 
+    load_blocks.wait()
     with jax.named_scope("relay_and_mix"):
         for q in range(max(half, NODES)):
             if q < half:
@@ -131,6 +137,7 @@
     with jax.named_scope("tau"):
         for copy in tau_copies:
             copy.wait_recv()
+        load_tau.wait()
         whole = tau_in[...].astype(F32)
         tau_real = whole[:, 0].reshape(order, order).T
         tau_imag = whole[:, 1].reshape(order, order).T
@@ -232,9 +239,11 @@
     out = pl.pallas_call(
         functools.partial(kernel, n_src, n_snk, mom, order),
         out_shape=jax.ShapeDtypeStruct((n_src, planes, rows, order), BF16),
-        in_specs=[pl.BlockSpec(memory_space=pltpu.VMEM)] * 7,
+        in_specs=[pl.BlockSpec(memory_space=pltpu.HBM)] * 2
+        + [pl.BlockSpec(memory_space=pltpu.VMEM)] * 5,
         out_specs=pl.BlockSpec(memory_space=pltpu.VMEM),
         scratch_shapes=[
+            pltpu.VMEM((2 * mom, order, order), BF16),
             pltpu.VMEM((n_snk, 2, rows, order), BF16),
             pltpu.VMEM((2 * mom, order, order), BF16),
             pltpu.VMEM((2, NODES * mom * mom, order), F32),
@@ -251,6 +260,7 @@
             dma((n_src - 1,)), dma((n_src - 1,)),
             dma((n_snk - 1,)), dma((n_snk - 1,)),
             dma((n_src - 1,)), dma((n_src - 1,)),
+            dma((3,)),
         ],
         compiler_params=pltpu.CompilerParams(
             collective_id=0, has_side_effects=True, vmem_limit_bytes=40 * 2**20

time: 57.1 us -> 57.3 us (level)
  no operation moved by 1% of the time
where the time goes in v3:
time: 57.3 us; the launch traced here: 57.1 us
  Pallas kernels  52.7 us (92%)
  local copies, waits for them, and re-layouts  4.34 us (8%)
    pallas_call x1, Pallas kernels, shards(): pl.pallas_call(functools.partial(kernel, n_src, n_snk, mom, order), out_s...  52.7 us
    unnamed x15, local copies, waits for them, and re-layouts  3.55 us

profile of v3, /device:TPU:29, one launch (start us, length us, event | category | flops | bytes accessed | tf_op | source)
XLA Modules:
  0.0 57.1 jit_solution(16588990376213146651)
XLA Ops:
  0.0 0.0 copy-start.6
  0.0 0.7 %copy-done.6 = f32[16,2]{0,1:T(2,128)S(1)} copy-done((f32[16,2]{0,1:T(2,128)S(1)}, f32[16,2]{0,1:T(2,128)}, u32[]{:S(2)}) %copy-start.6) | copy-done | bytes 152
  0.7 0.0 copy-start.2
  0.7 0.0 copy-start.3
  0.7 0.0 copy-start.4
  0.7 0.0 copy-start.5
  0.7 0.1 copy.8.table_ref
  0.8 0.6 copy-done.2
  1.3 0.0 copy-done.3
  1.4 0.0 copy-done.4
  1.4 0.0 copy-done.5
  1.4 0.0 copy-start
  1.4 1.2 %copy-done = bf16[1,4,2,256,256]{4,3,2,1,0:T(8,128)(2,1)S(1)} copy-done((bf16[1,4,2,256,256]{4,3,2,1,0:T(8,128)(2,1)S(1)}, bf16[1,4,2,256,256]{4,3,2,1,0:T(8,128)(2,1)}, u32[]{:S(2)}) %copy-start) | copy-done | bytes 1048600
  2.6 0.0 copy-start.1
  2.6 0.9 %copy-done.1 = bf16[1,8,2,256,32]{3,4,2,1,0:T(8,128)(2,1)S(1)} copy-done((bf16[1,8,2,256,32]{3,4,2,1,0:T(8,128)(2,1)S(1)}, bf16[1,8,2,256,32]{3,4,2,1,0:T(8,128)(2,1)}, u32[]{:S(2)}) %copy-start.1) | copy-done | bytes 262168
  3.6 52.7 %shard_map.73 = bf16[4,2,32,256]{3,2,1,0:T(8,128)(2,1)S(1)} custom-call(bf16[8,2,32,256]{3,2,1,0:T(8,128)(2,1)S(1)} %bitcast.11, bf16[8,256,256]{2,1,0:T(8,128)(2,1)S(1)} %bitcast.9, s32[1,32]{1,0:T(1,128)S(1)} %bitcast.12, s32[1,32]{1,0:T(1,128)S(1)} %bitcast.13, s32[1,32]{1,0:T(1,128)S(1)} %bitcast.14, s32[1,32]{1,0:T(1,128)S(1)} %bitcast.15, ...), custom_call_target="tpu_custom_call" | custom-call | tf_op jit(solution)/shard_map/pallas_call | solution.py:239
  56.3 0.8 %copy.9 = bf16[32,4,2,256]{3,2,1,0:T(2,128)(2,1)} copy(bf16[32,4,2,256]{3,0,2,1:T(8,128)(2,1)S(1)} %bitcast.10) | data formatting | bytes 262144 | tf_op jit(solution)/shard_map/transpose | solution.py:270
Async XLA Ops:
  0.0 0.7 %copy-start.6 = (f32[16,2]{0,1:T(2,128)S(1)}, f32[16,2]{0,1:T(2,128)}, u32[]{:S(2)}) copy-start(f32[16,2]{0,1:T(2,128)} %param.13) | copy-start | bytes 388
  0.7 0.7 %copy-start.2 = (s32[1,1,32]{2,1,0:T(1,128)S(1)}, s32[1,1,32]{2,1,0:T(1,128)}, u32[]{:S(2)}) copy-start(s32[1,1,32]{2,1,0:T(1,128)} %param.9) | copy-start | bytes 388
  0.7 0.7 %copy-start.3 = (s32[1,1,32]{2,1,0:T(1,128)S(1)}, s32[1,1,32]{2,1,0:T(1,128)}, u32[]{:S(2)}) copy-start(s32[1,1,32]{2,1,0:T(1,128)} %param.10) | copy-start | bytes 388
  0.7 0.7 %copy-start.4 = (s32[1,1,32]{2,1,0:T(1,128)S(1)}, s32[1,1,32]{2,1,0:T(1,128)}, u32[]{:S(2)}) copy-start(s32[1,1,32]{2,1,0:T(1,128)} %param.11) | copy-start | bytes 388
  0.7 0.7 %copy-start.5 = (s32[1,1,32]{2,1,0:T(1,128)S(1)}, s32[1,1,32]{2,1,0:T(1,128)}, u32[]{:S(2)}) copy-start(s32[1,1,32]{2,1,0:T(1,128)} %param.12) | copy-start | bytes 388
  1.4 1.2 %copy-start = (bf16[1,4,2,256,256]{4,3,2,1,0:T(8,128)(2,1)S(1)}, bf16[1,4,2,256,256]{4,3,2,1,0:T(8,128)(2,1)}, u32[]{:S(2)}) copy-start(bf16[1,4,2,256,256]{4,3,2,1,0:T(8,128)(2,1)} %param.8) | copy-start | bytes 3145732
  2.6 0.9 %copy-start.1 = (bf16[1,8,2,256,32]{3,4,2,1,0:T(8,128)(2,1)S(1)}, bf16[1,8,2,256,32]{3,4,2,1,0:T(8,128)(2,1)}, u32[]{:S(2)}) copy-start(bf16[1,8,2,256,32]{3,4,2,1,0:T(8,128)(2,1)} %param.7) | copy-start | bytes 786436

commit v4 on v1

--- a/solution.py
+++ b/solution.py
@@ -77,7 +77,11 @@
         for piece in range(2 * mom):
             right_buf[piece] = blocks_ref[piece]
         for q in range(half):
+            for taken, copy in cast_ways(q)[:2]:
+                pl.when(taken)(copy.start)
             cast_rest(q).start()
+        for q in range(half):
+            cast_ways(q)[2][1].start()
 
     tau_copies = []
     for d in range(1, n_snk):
@@ -124,7 +128,7 @@
             if q < half:
                 cast_arrived(low * half + q)
                 for taken, copy in cast_ways(q):
-                    pl.when(taken)(copy.start)
+                    pl.when(taken & jnp.logical_not(is_root))(copy.start)
             if q < NODES:
                 mix_node(q)
 

time: 57.1 us -> 56 us (0.981)
  Pallas kernels: 52.2 us -> 51.5 us
    pallas_call x1, Pallas kernels: 52.2 us -> 51.5 us  [shards(): pl.pallas_call(functools.partial(kernel, n_src, n_snk, mom, order), out_s...]
where the time goes in v4:
time: 56 us; the launch traced here: 55.8 us
  Pallas kernels  51.5 us (92%)
  local copies, waits for them, and re-layouts  4.34 us (8%)
    pallas_call x1, Pallas kernels, shards(): pl.pallas_call(functools.partial(kernel, n_src, n_snk, mom, order), out_s...  51.5 us
    unnamed x15, local copies, waits for them, and re-layouts  3.55 us

profile of v4, /device:TPU:29, one launch (start us, length us, event | category | flops | bytes accessed | tf_op | source)
XLA Modules:
  0.0 55.8 jit_solution(11687659284691162336)
XLA Ops:
  0.0 0.0 copy-start.6
  0.0 0.7 %copy-done.6 = f32[16,2]{0,1:T(2,128)S(1)} copy-done((f32[16,2]{0,1:T(2,128)S(1)}, f32[16,2]{0,1:T(2,128)}, u32[]{:S(2)}) %copy-start.6) | copy-done | bytes 152
  0.7 0.0 copy-start.2
  0.7 0.0 copy-start.3
  0.7 0.0 copy-start.4
  0.7 0.0 copy-start.5
  0.7 0.1 copy.8.table_ref
  0.8 0.6 %copy-done.2 = s32[1,1,32]{2,1,0:T(1,128)S(1)} copy-done((s32[1,1,32]{2,1,0:T(1,128)S(1)}, s32[1,1,32]{2,1,0:T(1,128)}, u32[]{:S(2)}) %copy-start.2) | copy-done | bytes 152
  1.3 0.0 copy-done.3
  1.4 0.0 copy-done.4
  1.4 0.0 copy-done.5
  1.4 0.0 copy-start
  1.4 1.2 %copy-done = bf16[1,4,2,256,256]{4,3,2,1,0:T(8,128)(2,1)S(1)} copy-done((bf16[1,4,2,256,256]{4,3,2,1,0:T(8,128)(2,1)S(1)}, bf16[1,4,2,256,256]{4,3,2,1,0:T(8,128)(2,1)}, u32[]{:S(2)}) %copy-start) | copy-done | bytes 1048600
  2.6 0.0 copy-start.1
  2.6 0.9 %copy-done.1 = bf16[1,8,2,256,32]{3,4,2,1,0:T(8,128)(2,1)S(1)} copy-done((bf16[1,8,2,256,32]{3,4,2,1,0:T(8,128)(2,1)S(1)}, bf16[1,8,2,256,32]{3,4,2,1,0:T(8,128)(2,1)}, u32[]{:S(2)}) %copy-start.1) | copy-done | bytes 262168
  3.6 51.5 %shard_map.73 = bf16[4,2,32,256]{3,2,1,0:T(8,128)(2,1)S(1)} custom-call(bf16[8,2,32,256]{3,2,1,0:T(8,128)(2,1)S(1)} %bitcast.11, bf16[8,256,256]{2,1,0:T(8,128)(2,1)S(1)} %bitcast.9, s32[1,32]{1,0:T(1,128)S(1)} %bitcast.12, s32[1,32]{1,0:T(1,128)S(1)} %bitcast.13, s32[1,32]{1,0:T(1,128)S(1)} %bitcast.14, s32[1,32]{1,0:T(1,128)S(1)} %bitcast.15, ...), custom_call_target="tpu_custom_call" | custom-call | tf_op jit(solution)/shard_map/pallas_call | solution.py:236
  55.0 0.8 %copy.9 = bf16[32,4,2,256]{3,2,1,0:T(2,128)(2,1)} copy(bf16[32,4,2,256]{3,0,2,1:T(8,128)(2,1)S(1)} %bitcast.10) | data formatting | bytes 262144 | tf_op jit(solution)/shard_map/transpose | solution.py:264
Async XLA Ops:
  0.0 0.7 %copy-start.6 = (f32[16,2]{0,1:T(2,128)S(1)}, f32[16,2]{0,1:T(2,128)}, u32[]{:S(2)}) copy-start(f32[16,2]{0,1:T(2,128)} %param.13) | copy-start | bytes 388
  0.7 0.7 %copy-start.2 = (s32[1,1,32]{2,1,0:T(1,128)S(1)}, s32[1,1,32]{2,1,0:T(1,128)}, u32[]{:S(2)}) copy-start(s32[1,1,32]{2,1,0:T(1,128)} %param.9) | copy-start | bytes 388
  0.7 0.7 %copy-start.3 = (s32[1,1,32]{2,1,0:T(1,128)S(1)}, s32[1,1,32]{2,1,0:T(1,128)}, u32[]{:S(2)}) copy-start(s32[1,1,32]{2,1,0:T(1,128)} %param.10) | copy-start | bytes 388
  0.7 0.7 %copy-start.4 = (s32[1,1,32]{2,1,0:T(1,128)S(1)}, s32[1,1,32]{2,1,0:T(1,128)}, u32[]{:S(2)}) copy-start(s32[1,1,32]{2,1,0:T(1,128)} %param.11) | copy-start | bytes 388
  0.7 0.7 %copy-start.5 = (s32[1,1,32]{2,1,0:T(1,128)S(1)}, s32[1,1,32]{2,1,0:T(1,128)}, u32[]{:S(2)}) copy-start(s32[1,1,32]{2,1,0:T(1,128)} %param.12) | copy-start | bytes 388
  1.4 1.2 %copy-start = (bf16[1,4,2,256,256]{4,3,2,1,0:T(8,128)(2,1)S(1)}, bf16[1,4,2,256,256]{4,3,2,1,0:T(8,128)(2,1)}, u32[]{:S(2)}) copy-start(bf16[1,4,2,256,256]{4,3,2,1,0:T(8,128)(2,1)} %param.8) | copy-start | bytes 3145732
  2.6 0.9 %copy-start.1 = (bf16[1,8,2,256,32]{3,4,2,1,0:T(8,128)(2,1)S(1)}, bf16[1,8,2,256,32]{3,4,2,1,0:T(8,128)(2,1)}, u32[]{:S(2)}) copy-start(bf16[1,8,2,256,32]{3,4,2,1,0:T(8,128)(2,1)} %param.7) | copy-start | bytes 786436

commit v5 on v4

--- a/solution.py
+++ b/solution.py
@@ -36,6 +36,14 @@
     goes_up = (high >= root_high) & (high + 1 < n_snk // 2)
     goes_down = (high <= root_high) & (high >= 1)
 
+    assist = lax.rem(s + n_src // 2, n_src)
+    assist_root = assist * (n_snk // n_src)
+    assist_low = assist_root % 2
+    assist_pair = assist_root + 1 - 2 * assist_low
+    is_helper = t == assist_root
+    is_pair = (high == root_high) & (low != root_low)
+    own_pair = half // 2
+
     def snk_peer(d):
         return lax.rem(t + d, n_snk)
 
@@ -47,7 +55,20 @@
         pl.semaphore_signal(barrier, inc=1, device_id=(s, snk_peer(d)), device_id_type=MESH)
     for d in range(1, n_src):
         pl.semaphore_signal(barrier, inc=1, device_id=(src_peer(d), t), device_id_type=MESH)
-    pl.semaphore_wait(barrier, n_snk + n_src - 2)
+
+    @pl.when(is_pair)
+    def _():
+        pl.semaphore_signal(barrier, inc=1, device_id=(assist, root), device_id_type=MESH)
+
+    pl.semaphore_wait(barrier, n_snk + n_src - 2 + is_helper.astype(jnp.int32))
+
+    def help_pair(q):
+        piece = assist_low * half + q
+        return pltpu.make_async_remote_copy(
+            src_ref=blocks_ref.at[piece], dst_ref=right_buf.at[piece],
+            send_sem=cast_send.at[4, q], recv_sem=cast_recv.at[piece],
+            device_id=(assist, assist_pair), device_id_type=MESH,
+        )
 
     def cast(piece, kind, q, target):
         return pltpu.make_async_remote_copy(
@@ -61,7 +82,7 @@
         return (
             (goes_up, cast(mine, 0, q, jnp.minimum(t + 2, n_snk - 1))),
             (goes_down, cast(mine, 1, q, jnp.maximum(t - 2, 0))),
-            (jnp.logical_not(pair_is_root), cast(mine, 2, q, high * 2 + other)),
+            (jnp.logical_not(pair_is_root) & (jnp.logical_not(is_root) | (q < own_pair)), cast(mine, 2, q, high * 2 + other)),
         )
 
     def cast_rest(q):
@@ -80,8 +101,13 @@
             for taken, copy in cast_ways(q)[:2]:
                 pl.when(taken)(copy.start)
             cast_rest(q).start()
-        for q in range(half):
+        for q in range(own_pair):
             cast_ways(q)[2][1].start()
+
+    @pl.when(is_helper)
+    def _():
+        for q in range(own_pair, half):
+            help_pair(q).start()
 
     tau_copies = []
     for d in range(1, n_snk):
@@ -221,6 +247,8 @@
         for taken, copy in cast_ways(q):
             pl.when(taken)(copy.wait_send)
         pl.when(is_root)(cast_rest(q).wait_send)
+        if q >= own_pair:
+            pl.when(is_helper)(help_pair(q).wait_send)
     for copy in tau_copies + part_copies + share_copies + done_copies:
         copy.wait_send()
 
@@ -251,7 +279,7 @@
             pltpu.VMEM((n_snk - 1, planes, rows, order), BF16),
             pltpu.VMEM((n_src, planes, rows, order), BF16),
             dma((n_snk - 1,)), dma((n_snk - 1,)),
-            dma((4, mom)), dma((2 * mom,)),
+            dma((5, mom)), dma((2 * mom,)),
             dma((n_src - 1,)), dma((n_src - 1,)),
             dma((n_snk - 1,)), dma((n_snk - 1,)),
             dma((n_src - 1,)), dma((n_src - 1,)),

time: 56 us -> 56.1 us (level)
  no operation moved by 1% of the time
where the time goes in v5:
time: 56.1 us; the launch traced here: 55.9 us
  Pallas kernels  51.6 us (92%)
  local copies, waits for them, and re-layouts  4.34 us (8%)
    pallas_call x1, Pallas kernels, shards(): pl.pallas_call(functools.partial(kernel, n_src, n_snk, mom, order), out_s...  51.6 us
    unnamed x15, local copies, waits for them, and re-layouts  3.55 us

profile of v5, /device:TPU:29, one launch (start us, length us, event | category | flops | bytes accessed | tf_op | source)
XLA Modules:
  0.0 55.9 jit_solution(1073438371262445662)
XLA Ops:
  0.0 0.0 copy-start.6
  0.0 0.7 %copy-done.6 = f32[16,2]{0,1:T(2,128)S(1)} copy-done((f32[16,2]{0,1:T(2,128)S(1)}, f32[16,2]{0,1:T(2,128)}, u32[]{:S(2)}) %copy-start.6) | copy-done | bytes 152
  0.7 0.0 copy-start.2
  0.7 0.0 copy-start.3
  0.7 0.0 copy-start.4
  0.7 0.0 copy-start.5
  0.7 0.1 copy.8.table_ref
  0.8 0.6 %copy-done.2 = s32[1,1,32]{2,1,0:T(1,128)S(1)} copy-done((s32[1,1,32]{2,1,0:T(1,128)S(1)}, s32[1,1,32]{2,1,0:T(1,128)}, u32[]{:S(2)}) %copy-start.2) | copy-done | bytes 152
  1.3 0.0 copy-done.3
  1.4 0.0 copy-done.4
  1.4 0.0 copy-done.5
  1.4 0.0 copy-start
  1.4 1.2 %copy-done = bf16[1,4,2,256,256]{4,3,2,1,0:T(8,128)(2,1)S(1)} copy-done((bf16[1,4,2,256,256]{4,3,2,1,0:T(8,128)(2,1)S(1)}, bf16[1,4,2,256,256]{4,3,2,1,0:T(8,128)(2,1)}, u32[]{:S(2)}) %copy-start) | copy-done | bytes 1048600
  2.6 0.0 copy-start.1
  2.6 0.9 %copy-done.1 = bf16[1,8,2,256,32]{3,4,2,1,0:T(8,128)(2,1)S(1)} copy-done((bf16[1,8,2,256,32]{3,4,2,1,0:T(8,128)(2,1)S(1)}, bf16[1,8,2,256,32]{3,4,2,1,0:T(8,128)(2,1)}, u32[]{:S(2)}) %copy-start.1) | copy-done | bytes 262168
  3.6 51.6 %shard_map.73 = bf16[4,2,32,256]{3,2,1,0:T(8,128)(2,1)S(1)} custom-call(bf16[8,2,32,256]{3,2,1,0:T(8,128)(2,1)S(1)} %bitcast.11, bf16[8,256,256]{2,1,0:T(8,128)(2,1)S(1)} %bitcast.9, s32[1,32]{1,0:T(1,128)S(1)} %bitcast.12, s32[1,32]{1,0:T(1,128)S(1)} %bitcast.13, s32[1,32]{1,0:T(1,128)S(1)} %bitcast.14, s32[1,32]{1,0:T(1,128)S(1)} %bitcast.15, ...), custom_call_target="tpu_custom_call" | custom-call | tf_op jit(solution)/shard_map/pallas_call | solution.py:264
  55.1 0.8 %copy.9 = bf16[32,4,2,256]{3,2,1,0:T(2,128)(2,1)} copy(bf16[32,4,2,256]{3,0,2,1:T(8,128)(2,1)S(1)} %bitcast.10) | data formatting | bytes 262144 | tf_op jit(solution)/shard_map/transpose | solution.py:292
Async XLA Ops:
  0.0 0.7 %copy-start.6 = (f32[16,2]{0,1:T(2,128)S(1)}, f32[16,2]{0,1:T(2,128)}, u32[]{:S(2)}) copy-start(f32[16,2]{0,1:T(2,128)} %param.13) | copy-start | bytes 388
  0.7 0.7 %copy-start.2 = (s32[1,1,32]{2,1,0:T(1,128)S(1)}, s32[1,1,32]{2,1,0:T(1,128)}, u32[]{:S(2)}) copy-start(s32[1,1,32]{2,1,0:T(1,128)} %param.9) | copy-start | bytes 388
  0.7 0.7 %copy-start.3 = (s32[1,1,32]{2,1,0:T(1,128)S(1)}, s32[1,1,32]{2,1,0:T(1,128)}, u32[]{:S(2)}) copy-start(s32[1,1,32]{2,1,0:T(1,128)} %param.10) | copy-start | bytes 388
  0.7 0.7 %copy-start.4 = (s32[1,1,32]{2,1,0:T(1,128)S(1)}, s32[1,1,32]{2,1,0:T(1,128)}, u32[]{:S(2)}) copy-start(s32[1,1,32]{2,1,0:T(1,128)} %param.11) | copy-start | bytes 388
  0.7 0.7 %copy-start.5 = (s32[1,1,32]{2,1,0:T(1,128)S(1)}, s32[1,1,32]{2,1,0:T(1,128)}, u32[]{:S(2)}) copy-start(s32[1,1,32]{2,1,0:T(1,128)} %param.12) | copy-start | bytes 388
  1.4 1.2 %copy-start = (bf16[1,4,2,256,256]{4,3,2,1,0:T(8,128)(2,1)S(1)}, bf16[1,4,2,256,256]{4,3,2,1,0:T(8,128)(2,1)}, u32[]{:S(2)}) copy-start(bf16[1,4,2,256,256]{4,3,2,1,0:T(8,128)(2,1)} %param.8) | copy-start | bytes 3145732
  2.6 0.9 %copy-start.1 = (bf16[1,8,2,256,32]{3,4,2,1,0:T(8,128)(2,1)S(1)}, bf16[1,8,2,256,32]{3,4,2,1,0:T(8,128)(2,1)}, u32[]{:S(2)}) copy-start(bf16[1,8,2,256,32]{3,4,2,1,0:T(8,128)(2,1)} %param.7) | copy-start | bytes 786436
